TPU v7x, 256 devices: a whole 4x4x8 slice. The times are simulated.
256 devices in a mesh: gx: 32 (over z, y_lo, core), gy: 8 (over y_hi, x).
Axes of the slice: x: 4, y: 4 (y_hi: 2, y_lo: 2; y = y_hi * 2 + y_lo), z: 8, core: 2. Of those that a mesh axis runs over, the one named last changes fastest.
Arguments:
- image_tile: bfloat16 [256, 2048, 128], P('gy', 'gx'), may hold values from -6 to 6
- cotangent: bfloat16 [256, 2048, 128], P('gy', 'gx'), may hold values from -6 to 6
- weights: bfloat16 [3, 3, 3, 128, 128], replicated, may hold values from -0.1875 to 0.1875
Outputs:
- features: bfloat16 [256, 2048, 128], P('gy', 'gx')
- image_grad: bfloat16 [256, 2048, 128], P('gy', 'gx')
- weight_grad: float32 [3, 3, 3, 128, 128], replicated
All inputs are finite; a program needn't handle non-finite values.
Results may differ from a plain program's by a relative error of at most 0.008.
Values may be sent and summed in bfloat16 or wider, within the bound.
A program may use at most 128 MiB of HBM per device.

v0:
```python
import math

import jax
import jax.numpy as jnp
from jax import lax
from jax.sharding import PartitionSpec as P


def with_halo(cells, sides, width):
    for axis, dim in sides:
        count = lax.axis_size(axis)
        ends = count - 1
        head = lax.slice_in_dim(cells, 0, width, axis=dim)
        tail = lax.slice_in_dim(cells, cells.shape[dim] - width, cells.shape[dim], axis=dim)
        cells = jnp.concatenate(
            [
                lax.ppermute(tail, axis, [(i, (i + 1) % count) for i in range(ends)]),
                cells,
                lax.ppermute(head, axis, [((i + 1) % count, i) for i in range(ends)]),
            ],
            axis=dim,
        )
    return cells


def from_behind(block, axis, distance):
    devices = range(lax.axis_size(axis))
    route = [(i - distance, i) for i in devices if i - distance in devices]
    return lax.ppermute(block, axis, route)


def row_section(source, dilation):
    row_count = source.shape[0]
    if dilation <= row_count:
        return (with_halo(source, (("gy", 0),), dilation), dilation)
    hop_count = dilation // row_count
    lower_rows = from_behind(source, "gy", hop_count)
    top_border_rows = from_behind(source, "gy", -hop_count)
    return (jnp.concatenate([lower_rows, source, top_border_rows], axis=0), row_count)


def col_section(source, dilation):
    col_count = source.shape[1]
    if dilation < col_count:
        return (with_halo(source, (("gx", 1),), dilation), dilation)
    hop_count = dilation // col_count
    lower_cols = from_behind(source, "gx", hop_count)
    upper_cols = from_behind(source, "gx", -hop_count)
    return (jnp.concatenate([lower_cols, source, upper_cols], axis=1), col_count)


def gather_taps(extended, row_stride, col_step, row_count, col_count, channels):
    tap_list = [
        extended[
            i * row_stride : i * row_stride + row_count, j * col_step : j * col_step + col_count
        ]
        for i in range(3)
        for j in range(3)
    ]
    return jnp.stack(tap_list, axis=2).reshape(row_count * col_count, 9 * channels)


def spread(source, dilation):
    row_count, col_count, channels = source.shape
    row_ext, row_stride = row_section(source, dilation)
    extended, col_step = col_section(row_ext, dilation)
    return gather_taps(extended, row_stride, col_step, row_count, col_count, channels)


def shards(image_tile, cotangent, weights):
    row_count, col_count, channels = image_tile.shape
    layer_count = weights.shape[0]
    grid_width_count = lax.axis_size("gx")
    grid_height_count = lax.axis_size("gy")
    initial_dilation = max(grid_width_count, grid_height_count)
    dilation_rates = [initial_dilation, 2 * initial_dilation, 4 * initial_dilation]
    scale_factor = 1.0 / math.sqrt(row_count * col_count * grid_width_count * grid_height_count)
    hidden = image_tile
    hidden_list = []
    patch_list = []
    for k in range(layer_count):
        activated = jax.nn.elu(hidden.astype(jnp.float32)).astype(jnp.bfloat16)
        patches = spread(activated, dilation_rates[k])
        kernel = weights[k].reshape(9 * channels, channels)
        mixed = jnp.dot(patches, kernel, preferred_element_type=jnp.float32).reshape(
            row_count, col_count, channels
        )
        hidden_list.append(hidden)
        patch_list.append(patches)
        hidden = (hidden.astype(jnp.float32) + mixed).astype(jnp.bfloat16)
    upstream = cotangent.astype(jnp.float32)
    grad_list = [None] * layer_count
    for k in reversed(range(layer_count)):
        rounded = upstream.astype(jnp.bfloat16)
        partial_grad = lax.dot_general(
            patch_list[k],
            rounded.reshape(row_count * col_count, channels),
            (((0,), (0,)), ((), ())),
            preferred_element_type=jnp.float32,
        )
        grad_list[k] = partial_grad
        flipped = jnp.transpose(jnp.flip(weights[k], (0, 1)), (0, 1, 3, 2)).reshape(
            9 * channels, channels
        )
        back_term = jnp.dot(
            spread(rounded, dilation_rates[k]), flipped, preferred_element_type=jnp.float32
        ).reshape(row_count, col_count, channels)
        upstream = upstream + back_term * jnp.exp(
            jnp.minimum(hidden_list[k].astype(jnp.float32), 0.0)
        )
    stacked = jnp.stack(grad_list)
    stacked = lax.psum(stacked, ("gx", "gy"))
    weight_grad = (stacked * scale_factor).reshape(layer_count, 3, 3, channels, channels)
    grad_map = upstream.astype(jnp.bfloat16)
    return (hidden, grad_map, weight_grad)


def solution(mesh):
    placed = (P("gy", "gx", None), P("gy", "gx", None), P())
    return jax.shard_map(
        shards,
        mesh=mesh,
        in_specs=placed,
        out_specs=(P("gy", "gx", None), P("gy", "gx", None), P()),
        check_vma=False,
    )
```

profile of v0, /device:TPU:1, one launch (start us, length us, event | category | flops | bytes accessed | tf_op | source)
XLA Modules:
  0.0 666.5 jit_solution(278348843182350593)
XLA Ops:
  8.8 4.0 collective-permute-start
  14.1 9.3 %collective-permute-start.12 = (bf16[32,64,128]{2,1,0:T(8,128)(2,1)}, bf16[32,64,128]{2,1,0:T(8,128)(2,1)S(1)}, u32[]{:S(2)}, u32[]{:S(2)}) collective-permute-start(bf16[32,64,128]{2,1,0:T(8,128)(2,1)} %param.4), channel_id=1, source_target_pairs={{0,4},{1,5},{2,6},{3,7},{8,12},{9,13},{10,14},{11,15},{16,20},{17,... | collective-permute-start | bytes 1572872 | tf_op jit(solution)/shard_map/ppermute | solution.py:29
  23.4 3.7 collective-permute-done.1
  27.6 5.0 collective-permute-start.2
  35.9 3.7 collective-permute-done.12
  41.3 63.1 %collective-permute-done.13 = bf16[32,64,128]{2,1,0:T(8,128)(2,1)S(1)} collective-permute-done((bf16[32,64,128]{2,1,0:T(8,128)(2,1)S(1)}, bf16[32,64,128]{2,1,0:T(8,128)(2,1)S(1)}, u32[]{:S(2)}, u32[]{:S(2)}) %collective-permute-start.13) | collective-permute-done | bytes 524320 | tf_op jit(solution)/shard_map/ppermute | solution.py:29
  105.2 2.6 collective-permute-start.14
  110.3 2.7 fusion.78
  118.2 2.5 collective-permute-done.4
  120.7 11.1 %collective-permute-done.5 = bf16[32,64,128]{2,1,0:T(8,128)(2,1)S(1)} collective-permute-done((bf16[32,64,128]{2,1,0:T(8,128)(2,1)}, bf16[32,64,128]{2,1,0:T(8,128)(2,1)S(1)}, u32[]{:S(2)}, u32[]{:S(2)}) %collective-permute-start.5) | collective-permute-done | bytes 524320 | tf_op jit(solution)/shard_map/ppermute | solution.py:29
  135.0 2.5 collective-permute-start.7
  137.5 31.7 %collective-permute-done.14 = bf16[96,64,128]{2,1,0:T(8,128)(2,1)} collective-permute-done((bf16[96,64,128]{2,1,0:T(8,128)(2,1)}, bf16[96,64,128]{2,1,0:T(8,128)(2,1)}, u32[]{:S(2)}, u32[]{:S(2)}) %collective-permute-start.14) | collective-permute-done | bytes 1572896 | tf_op jit(solution)/shard_map/ppermute | solution.py:29
  176.2 15.4 %collective-permute-done.6 = bf16[96,64,128]{2,1,0:T(8,128)(2,1)S(1)} collective-permute-done((bf16[96,64,128]{2,1,0:T(8,128)(2,1)S(1)}, bf16[96,64,128]{2,1,0:T(8,128)(2,1)S(1)}, u32[]{:S(2)}, u32[]{:S(2)}) %collective-permute-start.6) | collective-permute-done | bytes 1572896 | tf_op jit(solution)/shard_map/ppermute | solution.py:29
  192.7 2.6 fusion.80
  195.3 2.5 fusion.124
  200.4 4.8 collective-permute-done.16
  205.1 5.4 collective-permute-done.17
  211.8 5.5 collective-permute-start.18
  229.3 11.5 %copy.8 = bf16[32,64,9,128]{3,2,1,0:T(8,128)(2,1)S(1)} copy(bf16[32,64,9,128]{3,1,0,2:T(8,128)(2,1)} %copy-done.1) | data formatting | bytes 9437184 | tf_op jit(solution)/shard_map/stack | solution.py:60
  240.8 23.7 %copy.11 = bf16[32,64,9,128]{3,2,1,0:T(8,128)(2,1)} copy(bf16[32,64,9,128]{3,1,0,2:T(8,128)(2,1)} %copy-done) | data formatting | bytes 9437184 | tf_op jit(solution)/shard_map/stack | solution.py:60
  264.5 5.3 fusion.30
  271.0 2.2 collective-permute-start.10
  281.5 2.4 fusion.125
  286.8 63.3 %collective-permute-done.10 = bf16[96,64,128]{2,1,0:T(8,128)(2,1)S(1)} collective-permute-done((bf16[96,64,128]{2,1,0:T(8,128)(2,1)S(1)}, bf16[96,64,128]{2,1,0:T(8,128)(2,1)S(1)}, u32[]{:S(2)}, u32[]{:S(2)}) %collective-permute-start.10) | collective-permute-done | bytes 1572896 | tf_op jit(solution)/shard_map/ppermute | solution.py:29
  358.1 14.8 %copy.14 = bf16[32,64,9,128]{3,2,1,0:T(8,128)(2,1)} copy(bf16[32,64,9,128]{3,1,0,2:T(8,128)(2,1)} %fusion.101) | data formatting | bytes 9437184 | tf_op jit(solution)/shard_map/stack | solution.py:60
  372.9 2.2 fusion.27
  375.1 5.3 fusion.33
  383.4 6.6 collective-permute-start.22
  390.1 4.5 fusion.66
  396.5 255.7 %all-reduce.2.cloned.1.call-done = f32[3,1152,128]{2,1,0:T(8,128)} async-done(((f32[3,1152,128]{2,1,0:T(8,128)}), f32[3,1152,128]{2,1,0:T(8,128)}) %all-reduce.2.cloned.1.call-update) | async-done | bytes 1769488 | tf_op jit(solution)/shard_map/psum | solution.py:112
  652.3 2.8 broadcast_multiply_fusion
  657.0 2.3 fusion.69
  (141 shorter events, 70.5 us)
Async XLA Ops:
  7.2 25.4 %copy-start.2 = (bf16[32,64,128]{2,1,0:T(8,128)(2,1)S(1)}, bf16[32,64,128]{2,1,0:T(8,128)(2,1)}, u32[]{:S(2)}) copy-start(bf16[32,64,128]{2,1,0:T(8,128)(2,1)} %param.4) | copy-start | bytes 1572868
  7.2 645.1 %all-reduce.2.cloned.1.call-start = ((), (), s32[]{:S(2)}) async-start(), calls=%async_computation | async-start | bytes 3538944 | tf_op jit(solution)/shard_map/psum | solution.py:112
  7.2 28.6 %copy-start.7 = (bf16[3,3,3,128,128]{4,3,2,1,0:T(8,128)(2,1)S(1)}, bf16[3,3,3,128,128]{4,3,2,1,0:T(8,128)(2,1)}, u32[]{:S(2)}) copy-start(bf16[3,3,3,128,128]{4,3,2,1,0:T(8,128)(2,1)} %param.5) | copy-start | bytes 2654212
  8.8 14.6 %collective-permute-start = (bf16[32,64,128]{2,1,0:T(8,128)(2,1)S(1)}, bf16[32,64,128]{2,1,0:T(8,128)(2,1)S(1)}, u32[]{:S(2)}, u32[]{:S(2)}) collective-permute-start(bf16[32,64,128]{2,1,0:T(8,128)(2,1)S(1)} %fusion.76), channel_id=1, source_target_pairs={{0,1},{1,2},{2,3},{3,4},{4,5},{5,6},{6,7},{8,9},{9,10},{10,11},{11... | collective-permute-start | bytes 1572872 | tf_op jit(solution)/shard_map/ppermute | solution.py:17
  12.8 14.4 %collective-permute-start.1 = (bf16[32,64,128]{2,1,0:T(8,128)(2,1)S(1)}, bf16[32,64,128]{2,1,0:T(8,128)(2,1)S(1)}, u32[]{:S(2)}, u32[]{:S(2)}) collective-permute-start(bf16[32,64,128]{2,1,0:T(8,128)(2,1)S(1)} %fusion.76), channel_id=1, source_target_pairs={{1,0},{2,1},{3,2},{4,3},{5,4},{6,5},{7,6},{9,8},{10,9},{11,10},{12... | collective-permute-start | bytes 1572872 | tf_op jit(solution)/shard_map/ppermute | solution.py:19
  14.1 25.5 %collective-permute-start.12 = (bf16[32,64,128]{2,1,0:T(8,128)(2,1)}, bf16[32,64,128]{2,1,0:T(8,128)(2,1)S(1)}, u32[]{:S(2)}, u32[]{:S(2)}) collective-permute-start(bf16[32,64,128]{2,1,0:T(8,128)(2,1)} %param.4), channel_id=1, source_target_pairs={{0,4},{1,5},{2,6},{3,7},{8,12},{9,13},{10,14},{11,15},{16,20},{17,... | collective-permute-start | bytes 1572872 | tf_op jit(solution)/shard_map/ppermute | solution.py:29
  27.6 81.5 %collective-permute-start.2 = (bf16[96,32,128]{2,1,0:T(8,128)(2,1)S(1)}, bf16[96,32,128]{2,1,0:T(8,128)(2,1)S(1)}, u32[]{:S(2)}, u32[]{:S(2)}) collective-permute-start(bf16[96,32,128]{2,1,0:T(8,128)(2,1)S(1)} %get-tuple-element.6), channel_id=1, source_target_pairs={{0,8},{8,16},{16,24},{24,32},{32,40},{40,48},{48,56},{56,64},{64,7... | collective-permute-start | bytes 2359304 | tf_op jit(solution)/shard_map/ppermute | solution.py:17
  32.6 71.8 %collective-permute-start.13 = (bf16[32,64,128]{2,1,0:T(8,128)(2,1)S(1)}, bf16[32,64,128]{2,1,0:T(8,128)(2,1)S(1)}, u32[]{:S(2)}, u32[]{:S(2)}) collective-permute-start(bf16[32,64,128]{2,1,0:T(8,128)(2,1)S(1)} %copy-done.2), channel_id=1, source_target_pairs={{4,0},{5,1},{6,2},{7,3},{12,8},{13,9},{14,10},{15,11},{20,16},{21,... | collective-permute-start | bytes 1572872 | tf_op jit(solution)/shard_map/ppermute | solution.py:29
  33.9 75.3 %collective-permute-start.3 = (bf16[96,32,128]{2,1,0:T(8,128)(2,1)S(1)}, bf16[96,32,128]{2,1,0:T(8,128)(2,1)S(1)}, u32[]{:S(2)}, u32[]{:S(2)}) collective-permute-start(bf16[96,32,128]{2,1,0:T(8,128)(2,1)S(1)} %get-tuple-element.5), channel_id=1, source_target_pairs={{8,0},{16,8},{24,16},{32,24},{40,32},{48,40},{56,48},{64,56},{72,6... | collective-permute-start | bytes 2359304 | tf_op jit(solution)/shard_map/ppermute | solution.py:19
  35.9 74.4 %copy-start.5 = (bf16[1,3,3,128,128]{4,3,2,1,0:T(8,128)(2,1)}, bf16[1,3,3,128,128]{4,3,2,1,0:T(8,128)(2,1)S(1)}, u32[]{:S(2)}) copy-start(bf16[1,3,3,128,128]{4,3,2,1,0:T(8,128)(2,1)S(1)} %get-tuple-element.7) | copy-start | bytes 884740
  35.9 156.8 %copy-start.6 = (bf16[1,3,3,128,128]{4,3,2,1,0:T(8,128)(2,1)}, bf16[1,3,3,128,128]{4,3,2,1,0:T(8,128)(2,1)S(1)}, u32[]{:S(2)}) copy-start(bf16[1,3,3,128,128]{4,3,2,1,0:T(8,128)(2,1)S(1)} %get-tuple-element.8) | copy-start | bytes 884740
  105.2 64.0 %collective-permute-start.14 = (bf16[96,64,128]{2,1,0:T(8,128)(2,1)}, bf16[96,64,128]{2,1,0:T(8,128)(2,1)}, u32[]{:S(2)}, u32[]{:S(2)}) collective-permute-start(bf16[96,64,128]{2,1,0:T(8,128)(2,1)} %constant_dynamic-update-slice_fusion), channel_id=1, source_target_pairs={{0,16},{8,24},{16,32},{24,40},{32,48},{40,56},{48,64},{56,72},{64,... | collective-permute-start | bytes 4718600 | tf_op jit(solution)/shard_map/ppermute | solution.py:29
  107.8 62.6 %collective-permute-start.15 = (bf16[96,64,128]{2,1,0:T(8,128)(2,1)}, bf16[96,64,128]{2,1,0:T(8,128)(2,1)}, u32[]{:S(2)}, u32[]{:S(2)}) collective-permute-start(bf16[96,64,128]{2,1,0:T(8,128)(2,1)} %constant_dynamic-update-slice_fusion), channel_id=1, source_target_pairs={{16,0},{24,8},{32,16},{40,24},{48,32},{56,40},{64,48},{72,56},{80,... | collective-permute-start | bytes 4718600 | tf_op jit(solution)/shard_map/ppermute | solution.py:29
  113.0 7.7 %collective-permute-start.4 = (bf16[32,64,128]{2,1,0:T(8,128)(2,1)}, bf16[32,64,128]{2,1,0:T(8,128)(2,1)S(1)}, u32[]{:S(2)}, u32[]{:S(2)}) collective-permute-start(bf16[32,64,128]{2,1,0:T(8,128)(2,1)} %get-tuple-element.10), channel_id=1, source_target_pairs={{0,2},{1,3},{2,4},{3,5},{4,6},{5,7},{8,10},{9,11},{10,12},{11,13},... | collective-permute-start | bytes 1572872 | tf_op jit(solution)/shard_map/ppermute | solution.py:29
  114.3 17.5 %collective-permute-start.5 = (bf16[32,64,128]{2,1,0:T(8,128)(2,1)}, bf16[32,64,128]{2,1,0:T(8,128)(2,1)S(1)}, u32[]{:S(2)}, u32[]{:S(2)}) collective-permute-start(bf16[32,64,128]{2,1,0:T(8,128)(2,1)} %get-tuple-element.10), channel_id=1, source_target_pairs={{2,0},{3,1},{4,2},{5,3},{6,4},{7,5},{10,8},{11,9},{12,10},{13,11},... | collective-permute-start | bytes 1572872 | tf_op jit(solution)/shard_map/ppermute | solution.py:29
  133.1 58.5 %collective-permute-start.6 = (bf16[96,64,128]{2,1,0:T(8,128)(2,1)S(1)}, bf16[96,64,128]{2,1,0:T(8,128)(2,1)S(1)}, u32[]{:S(2)}, u32[]{:S(2)}) collective-permute-start(bf16[96,64,128]{2,1,0:T(8,128)(2,1)S(1)} %pad_maximum_fusion.2), channel_id=1, source_target_pairs={{0,8},{8,16},{16,24},{24,32},{32,40},{40,48},{48,56},{56,64},{64,7... | collective-permute-start | bytes 4718600 | tf_op jit(solution)/shard_map/ppermute | solution.py:29
  135.0 56.7 %collective-permute-start.7 = (bf16[96,64,128]{2,1,0:T(8,128)(2,1)S(1)}, bf16[96,64,128]{2,1,0:T(8,128)(2,1)S(1)}, u32[]{:S(2)}, u32[]{:S(2)}) collective-permute-start(bf16[96,64,128]{2,1,0:T(8,128)(2,1)S(1)} %pad_maximum_fusion.2), channel_id=1, source_target_pairs={{8,0},{16,8},{24,16},{32,24},{40,32},{48,40},{56,48},{64,56},{72,6... | collective-permute-start | bytes 4718600 | tf_op jit(solution)/shard_map/ppermute | solution.py:29
  172.6 19.3 %copy-start.8 = (bf16[32,64,128]{2,1,0:T(8,128)(2,1)S(1)}, bf16[32,64,128]{2,1,0:T(8,128)(2,1)}, u32[]{:S(2)}) copy-start(bf16[32,64,128]{2,1,0:T(8,128)(2,1)} %get-tuple-element.11) | copy-start | bytes 1572868
  195.3 16.6 %copy-start.10 = (bf16[32,64,128]{2,1,0:T(8,128)(2,1)}, bf16[32,64,128]{2,1,0:T(8,128)(2,1)S(1)}, u32[]{:S(2)}) copy-start(bf16[32,64,128]{2,1,0:T(8,128)(2,1)S(1)} %get-tuple-element.13) | copy-start | bytes 1572868
  197.8 7.4 %collective-permute-start.16 = (bf16[32,64,128]{2,1,0:T(8,128)(2,1)S(1)}, bf16[32,64,128]{2,1,0:T(8,128)(2,1)S(1)}, u32[]{:S(2)}, u32[]{:S(2)}) collective-permute-start(bf16[32,64,128]{2,1,0:T(8,128)(2,1)S(1)} %get-tuple-element.14), channel_id=1, source_target_pairs={{0,2},{1,3},{2,4},{3,5},{4,6},{5,7},{8,10},{9,11},{10,12},{11,13},... | collective-permute-start | bytes 1572872 | tf_op jit(solution)/shard_map/ppermute | solution.py:29
  199.1 11.4 %collective-permute-start.17 = (bf16[32,64,128]{2,1,0:T(8,128)(2,1)S(1)}, bf16[32,64,128]{2,1,0:T(8,128)(2,1)S(1)}, u32[]{:S(2)}, u32[]{:S(2)}) collective-permute-start(bf16[32,64,128]{2,1,0:T(8,128)(2,1)S(1)} %get-tuple-element.14), channel_id=1, source_target_pairs={{2,0},{3,1},{4,2},{5,3},{6,4},{7,5},{10,8},{11,9},{12,10},{13,11},... | collective-permute-start | bytes 1572872 | tf_op jit(solution)/shard_map/ppermute | solution.py:29
  211.8 62.8 %collective-permute-start.18 = (bf16[96,64,128]{2,1,0:T(8,128)(2,1)}, bf16[96,64,128]{2,1,0:T(8,128)(2,1)}, u32[]{:S(2)}, u32[]{:S(2)}) collective-permute-start(bf16[96,64,128]{2,1,0:T(8,128)(2,1)} %pad_maximum_fusion.4), channel_id=1, source_target_pairs={{0,8},{8,16},{16,24},{24,32},{32,40},{40,48},{48,56},{56,64},{64,7... | collective-permute-start | bytes 4718600 | tf_op jit(solution)/shard_map/ppermute | solution.py:29
  217.4 58.4 %collective-permute-start.19 = (bf16[96,64,128]{2,1,0:T(8,128)(2,1)}, bf16[96,64,128]{2,1,0:T(8,128)(2,1)}, u32[]{:S(2)}, u32[]{:S(2)}) collective-permute-start(bf16[96,64,128]{2,1,0:T(8,128)(2,1)} %pad_maximum_fusion.4), channel_id=1, source_target_pairs={{8,0},{16,8},{24,16},{32,24},{40,32},{48,40},{56,48},{64,56},{72,6... | collective-permute-start | bytes 4718600 | tf_op jit(solution)/shard_map/ppermute | solution.py:29
  219.3 50.5 %collective-permute-start.8 = (bf16[32,64,128]{2,1,0:T(8,128)(2,1)}, bf16[32,64,128]{2,1,0:T(8,128)(2,1)S(1)}, u32[]{:S(2)}, u32[]{:S(2)}) collective-permute-start(bf16[32,64,128]{2,1,0:T(8,128)(2,1)} %get-tuple-element.12), channel_id=1, source_target_pairs={{0,4},{1,5},{2,6},{3,7},{8,12},{9,13},{10,14},{11,15},{16,20},{17,... | collective-permute-start | bytes 1572872 | tf_op jit(solution)/shard_map/ppermute | solution.py:29
  220.6 49.2 %collective-permute-start.9 = (bf16[32,64,128]{2,1,0:T(8,128)(2,1)}, bf16[32,64,128]{2,1,0:T(8,128)(2,1)S(1)}, u32[]{:S(2)}, u32[]{:S(2)}) collective-permute-start(bf16[32,64,128]{2,1,0:T(8,128)(2,1)} %get-tuple-element.12), channel_id=1, source_target_pairs={{4,0},{5,1},{6,2},{7,3},{12,8},{13,9},{14,10},{15,11},{20,16},{21,... | collective-permute-start | bytes 1572872 | tf_op jit(solution)/shard_map/ppermute | solution.py:29
  271.0 79.0 %collective-permute-start.10 = (bf16[96,64,128]{2,1,0:T(8,128)(2,1)S(1)}, bf16[96,64,128]{2,1,0:T(8,128)(2,1)S(1)}, u32[]{:S(2)}, u32[]{:S(2)}) collective-permute-start(bf16[96,64,128]{2,1,0:T(8,128)(2,1)S(1)} %pad_maximum_fusion.3), channel_id=1, source_target_pairs={{0,16},{8,24},{16,32},{24,40},{32,48},{40,56},{48,64},{56,72},{64,... | collective-permute-start | bytes 4718600 | tf_op jit(solution)/shard_map/ppermute | solution.py:29
  273.3 78.5 %collective-permute-start.11 = (bf16[96,64,128]{2,1,0:T(8,128)(2,1)S(1)}, bf16[96,64,128]{2,1,0:T(8,128)(2,1)S(1)}, u32[]{:S(2)}, u32[]{:S(2)}) collective-permute-start(bf16[96,64,128]{2,1,0:T(8,128)(2,1)S(1)} %pad_maximum_fusion.3), channel_id=1, source_target_pairs={{16,0},{24,8},{32,16},{40,24},{48,32},{56,40},{64,48},{72,56},{80,... | collective-permute-start | bytes 4718600 | tf_op jit(solution)/shard_map/ppermute | solution.py:29
  281.5 71.9 %copy-start.11 = (bf16[32,64,128]{2,1,0:T(8,128)(2,1)S(1)}, bf16[32,64,128]{2,1,0:T(8,128)(2,1)}, u32[]{:S(2)}) copy-start(bf16[32,64,128]{2,1,0:T(8,128)(2,1)} %copy-done.10) | copy-start | bytes 1572868
  284.0 97.9 %collective-permute-start.20 = (bf16[32,64,128]{2,1,0:T(8,128)(2,1)S(1)}, bf16[32,64,128]{2,1,0:T(8,128)(2,1)S(1)}, u32[]{:S(2)}, u32[]{:S(2)}) collective-permute-start(bf16[32,64,128]{2,1,0:T(8,128)(2,1)S(1)} %get-tuple-element.16), channel_id=1, source_target_pairs={{0,1},{1,2},{2,3},{3,4},{4,5},{5,6},{6,7},{8,9},{9,10},{10,11},{11... | collective-permute-start | bytes 1572872 | tf_op jit(solution)/shard_map/ppermute | solution.py:17
  285.3 96.5 %collective-permute-start.21 = (bf16[32,64,128]{2,1,0:T(8,128)(2,1)S(1)}, bf16[32,64,128]{2,1,0:T(8,128)(2,1)S(1)}, u32[]{:S(2)}, u32[]{:S(2)}) collective-permute-start(bf16[32,64,128]{2,1,0:T(8,128)(2,1)S(1)} %get-tuple-element.16), channel_id=1, source_target_pairs={{1,0},{2,1},{3,2},{4,3},{5,4},{6,5},{7,6},{9,8},{10,9},{11,10},{12... | collective-permute-start | bytes 1572872 | tf_op jit(solution)/shard_map/ppermute | solution.py:19
  383.4 271.7 %collective-permute-start.22 = (bf16[96,32,128]{2,1,0:T(8,128)(2,1)}, bf16[96,32,128]{2,1,0:T(8,128)(2,1)S(1)}, u32[]{:S(2)}, u32[]{:S(2)}) collective-permute-start(bf16[96,32,128]{2,1,0:T(8,128)(2,1)} %get-tuple-element.4), channel_id=1, source_target_pairs={{0,8},{8,16},{16,24},{24,32},{32,40},{40,48},{48,56},{56,64},{64,7... | collective-permute-start | bytes 2359304 | tf_op jit(solution)/shard_map/ppermute | solution.py:17
  394.6 260.6 %collective-permute-start.23 = (bf16[96,32,128]{2,1,0:T(8,128)(2,1)}, bf16[96,32,128]{2,1,0:T(8,128)(2,1)S(1)}, u32[]{:S(2)}, u32[]{:S(2)}) collective-permute-start(bf16[96,32,128]{2,1,0:T(8,128)(2,1)} %get-tuple-element.3), channel_id=1, source_target_pairs={{8,0},{16,8},{24,16},{32,24},{40,32},{48,40},{56,48},{64,56},{72,6... | collective-permute-start | bytes 2359304 | tf_op jit(solution)/shard_map/ppermute | solution.py:19
  (11 other events, 55.6 us)
Sparse Core Ops, SparseCore 0:
  381.9 270.2 all-reduce.1
where the time goes:
time: 677 us; the launch traced here: 667 us
  waiting for transfers between devices  460 us (68%)
  local copies, waits for them, and re-layouts  86.5 us (13%)
  starting transfers between devices  61.5 us (9%)
  matrix products  29.7 us (4%)
  between operations  15.3 us (2%)
  other arithmetic  13 us (2%)
    psum x1, waiting for transfers between devices, shards(): stacked = lax.psum(stacked, ('gx', 'gy'))  256 us
    ppermute x16, waiting for transfers between devices, from_behind(): return lax.ppermute(block, axis, route)  201 us
    another operation x7, local copies, waits for them, and re-layouts, gather_taps(): jnp.stack(tap_list, axis=2).reshape(row_count * col_count, 9 * channels)  53.1 us
    ppermute x16, starting transfers between devices, from_behind(): return lax.ppermute(block, axis, route)  38 us
    unnamed x76, local copies, waits for them, and re-layouts  25.7 us
    ppermute x4, starting transfers between devices, with_halo(): lax.ppermute(tail, axis, [(i, (i + 1) % count) for i in range(ends)])  16.9 us
  transfers between devices with their start and end apart: 25, of which 11 were waited for; matrix products, arithmetic and copies ran while one was open for 17% of the time, Pallas kernels for 0%

commit v1 on v0

v1 whole, which is shorter than its diff:
```python
import functools
import math

import jax
import jax.numpy as jnp
from jax import lax
from jax.experimental import pallas as pl
from jax.experimental.pallas import tpu as pltpu
from jax.sharding import PartitionSpec as P

SUB = 4
HALO = 224
STEPS = (1, 2, 4)
SLICE = 48


def pairs_of(step):
    return [(o, o + step) for o in range(8) if (o // step) % 2 == 0]


def wait_bytes(ref, sem):
    pltpu.make_async_copy(ref, ref, sem).wait()


def elu(h):
    v = h.astype(jnp.float32)
    return jnp.where(v > 0, v, jnp.exp(jnp.minimum(v, 0.0)) - 1.0).astype(jnp.bfloat16)


def kernel(
    rows, cols, planes, scale,
    image, cotangent, weights,
    feat_out, grad_out, wg_out,
    wv, ft, cf, cb,
    h0, a0, h1, a1, h2, a2, ct,
    u2, r1, u1, r0, feat, grad,
    wacc, rsb, rsr, zr, ags,
    w_sem, in_send, in_recv, z_send, z_recv, out_send, out_recv,
    rs_send, rs_recv, zz_send, zz_recv, ag_send, ag_recv,
):
    gx, gy = lax.axis_index("gx"), lax.axis_index("gy")
    z, c = gx // SUB, gx % SUB
    me = gy * SUB + c
    group = rows
    width = SUB * cols
    own = pl.ds(HALO, width)
    total = width + 2 * HALO

    def at(q):
        return {"gx": z * SUB + q % SUB, "gy": q // SUB}

    def at_plane(p):
        return {"gx": p * SUB + c, "gy": gy}

    w_copy = pltpu.make_async_copy(weights, wv, w_sem)
    w_copy.start()

    barrier = pltpu.get_barrier_semaphore()

    def greet(t, carry):
        pl.semaphore_signal(barrier, inc=1, device_id=at((me + t) % group), device_id_type=pl.DeviceIdType.MESH)
        return carry

    lax.fori_loop(1, group, greet, 0)

    def greet_plane(t, carry):
        pl.semaphore_signal(barrier, inc=1, device_id=at_plane((z + t) % planes), device_id_type=pl.DeviceIdType.MESH)
        return carry

    lax.fori_loop(1, planes, greet_plane, 0)
    pl.semaphore_wait(barrier, group - 1 + planes - 1)

    def send_in(source, ext, n):
        place = ext.at[gy, pl.ds(pl.multiple_of(HALO + c * cols, 32), cols)]

        def one(t, carry):
            q = (me + t) % group
            pltpu.make_async_remote_copy(
                src_ref=source.at[q], dst_ref=place, send_sem=in_send.at[n], recv_sem=in_recv.at[n],
                device_id=at(q), device_id_type=pl.DeviceIdType.MESH,
            ).start()
            return carry

        lax.fori_loop(1, group, one, 0)
        pltpu.make_async_copy(source.at[me], place, in_recv.at[n]).start()

    def send_halo(ext, n):
        @pl.when(z < planes - 1)
        def _():
            pltpu.make_async_remote_copy(
                src_ref=ext.at[:, pl.ds(width, HALO)], dst_ref=ext.at[:, pl.ds(0, HALO)],
                send_sem=z_send.at[n, 0], recv_sem=z_recv.at[n, 0],
                device_id=at_plane(z + 1), device_id_type=pl.DeviceIdType.MESH,
            ).start()

        @pl.when(z > 0)
        def _():
            pltpu.make_async_remote_copy(
                src_ref=ext.at[:, pl.ds(HALO, HALO)], dst_ref=ext.at[:, pl.ds(HALO + width, HALO)],
                send_sem=z_send.at[n, 1], recv_sem=z_recv.at[n, 1],
                device_id=at_plane(z - 1), device_id_type=pl.DeviceIdType.MESH,
            ).start()

    def wait_halo(ext, n):
        @pl.when(z > 0)
        def _():
            wait_bytes(ext.at[:, pl.ds(0, HALO)], z_recv.at[n, 0])

        @pl.when(z < planes - 1)
        def _():
            wait_bytes(ext.at[:, pl.ds(HALO + width, HALO)], z_recv.at[n, 1])

    def zero_edges(ext):
        @pl.when(z == 0)
        def _():
            ext[:, 0:HALO, :] = jnp.zeros((8, HALO, 128), ext.dtype)

        @pl.when(z == planes - 1)
        def _():
            ext[:, HALO + width :, :] = jnp.zeros((8, HALO, 128), ext.dtype)

    def send_out(block, out, n):
        def one(t, carry):
            q = (me + t) % group
            pltpu.make_async_remote_copy(
                src_ref=block.at[q // SUB, pl.ds(pl.multiple_of((q % SUB) * cols, 32), cols)], dst_ref=out.at[me],
                send_sem=out_send.at[n], recv_sem=out_recv.at[n],
                device_id=at(q), device_id_type=pl.DeviceIdType.MESH,
            ).start()
            return carry

        lax.fori_loop(1, group, one, 0)
        pltpu.make_async_copy(
            block.at[gy, pl.ds(pl.multiple_of(c * cols, 32), cols)], out.at[me], out_recv.at[n]
        ).start()

    send_in(image, h0, 0)
    zero_edges(h0)
    zero_edges(ct)

    w_copy.wait()

    def flip(n, carry):
        k, m = n // 9, n % 9
        i, j = m // 3, m % 3
        ft[k, i, j] = wv[k, 2 - i, 2 - j].astype(jnp.float32).T.astype(jnp.bfloat16)
        return carry

    lax.fori_loop(0, 27, flip, 0)
    for src, dst in ((wv, cf), (ft, cb)):
        for k in range(3):
            for j in range(3):
                base = j * 256
                dst[k, base : base + 128, 0:128] = src[k, 1, j]
                dst[k, base : base + 128, 128:256] = src[k, 0, j]
                dst[k, base + 128 : base + 256, 0:128] = src[k, 2, j]
                dst[k, base + 128 : base + 256, 128:256] = src[k, 1, j]

    wait_bytes(h0.at[:, own], in_recv.at[0])
    send_halo(h0, 0)
    send_in(cotangent, ct, 1)
    for a in range(8):
        a0[a, HALO : HALO + width, :] = elu(h0[a, HALO : HALO + width, :])
    wait_bytes(ct.at[:, own], in_recv.at[1])
    send_halo(ct, 1)
    wait_halo(h0, 0)
    for a in range(8):
        a0[a, 0:HALO, :] = elu(h0[a, 0:HALO, :])
        a0[a, HALO + width :, :] = elu(h0[a, HALO + width :, :])

    left_in = z > 0
    right_in = z < planes - 1

    def conv(src, both, single, k, lo, emit):
        step, d = STEPS[k], 32 * STEPS[k]
        chunks = [(HALO, width, None)]
        if lo < HALO:
            chunks = [(lo, HALO - lo, left_in), chunks[0], (HALO + width, HALO - lo, right_in)]
        for start, size, inside in chunks:
            def taps(which):
                parts = []
                for j in range(3):
                    at_col = start + (j - 1) * d
                    parts += [src[r, at_col : at_col + size, :] for r in which]
                return jnp.concatenate(parts, axis=1)

            for first, second in pairs_of(step):
                acc = jnp.dot(taps((first, second)), both[k], preferred_element_type=jnp.float32)
                one, two = acc[:, 0:128], acc[:, 128:256]
                if first - step >= 0:
                    one = one + jnp.dot(
                        taps((first - step,)), single[k, 0].reshape(384, 128), preferred_element_type=jnp.float32
                    )
                if second + step < 8:
                    two = two + jnp.dot(
                        taps((second + step,)), single[k, 2].reshape(384, 128), preferred_element_type=jnp.float32
                    )
                emit(first, start, size, inside, one)
                emit(second, start, size, inside, two)

    def forward(old, new, active):
        def emit(row, start, size, inside, value):
            hid = old[row, start : start + size, :].astype(jnp.float32) + value
            if inside is not None:
                hid = jnp.where(inside, hid, 0.0)
            hid = hid.astype(jnp.bfloat16)
            if active is None:
                new[row, start - HALO : start - HALO + size, :] = hid
            else:
                new[row, start : start + size, :] = hid
                active[row, start : start + size, :] = elu(hid)

        return emit

    def backward(old, hidden, new, rounded):
        def emit(row, start, size, inside, value):
            gate = jnp.exp(jnp.minimum(hidden[row, start : start + size, :].astype(jnp.float32), 0.0))
            up = old[row, start : start + size, :].astype(jnp.float32) + value * gate
            if inside is not None:
                up = jnp.where(inside, up, 0.0)
            if new is None:
                rounded[row, start - HALO : start - HALO + size, :] = up.astype(jnp.bfloat16)
            else:
                new[row, start : start + size, :] = up
                rounded[row, start : start + size, :] = up.astype(jnp.bfloat16)

        return emit

    def kernel_grad(k, active, rounded):
        step, d = STEPS[k], 32 * STEPS[k]
        runs = [(0, step, 0, 2), (step, 8 - step, 0, 3), (8 - step, 8, 1, 3)]
        wacc[...] = jnp.zeros_like(wacc)
        for q0, q1, i0, i1 in runs:
            if q1 <= q0:
                continue
            count = (q1 - q0) * width
            left = jnp.concatenate(
                [
                    active[q0:q1, HALO + (j - 1) * d : HALO + (j - 1) * d + width, :].reshape(count, 128)
                    for j in range(3)
                ],
                axis=1,
            )
            right = jnp.concatenate(
                [
                    rounded[q0 - (i - 1) * step : q1 - (i - 1) * step, HALO : HALO + width, :].reshape(count, 128)
                    for i in range(i0, i1)
                ],
                axis=1,
            )
            wacc[:, i0 * 128 : i1 * 128] += lax.dot_general(
                left, right, (((0,), (0,)), ((), ())), preferred_element_type=jnp.float32
            )
        for i in range(3):
            for j in range(3):
                rsb[k, (i * 3 + j) * 128 : (i * 3 + j + 1) * 128, :] = wacc[
                    j * 128 : (j + 1) * 128, i * 128 : (i + 1) * 128
                ].astype(jnp.bfloat16)

        def one(t, carry):
            q = (me + t) % group

            @pl.when(q < reducers)
            def _():
                pltpu.make_async_remote_copy(
                    src_ref=rsb.at[k, pl.ds(pl.multiple_of(q * SLICE, 16), SLICE)], dst_ref=rsr.at[k, me],
                    send_sem=rs_send.at[k], recv_sem=rs_recv.at[k],
                    device_id=at(q), device_id_type=pl.DeviceIdType.MESH,
                ).start()

            return carry

        lax.fori_loop(1, group, one, 0)

        @pl.when(me < reducers)
        def _():
            pltpu.make_async_copy(
                rsb.at[k, pl.ds(pl.multiple_of(me * SLICE, 16), SLICE)], rsr.at[k, me], rs_recv.at[k]
            ).start()

    reducers = 9 * 128 // SLICE

    def sum_plane(k):
        @pl.when(me < reducers)
        def _():
            wait_bytes(rsr.at[k], rs_recv.at[k])
            part = rsr[k, 0].astype(jnp.float32)
            for n in range(1, group):
                part = part + rsr[k, n].astype(jnp.float32)
            zr[k, z] = part.astype(jnp.bfloat16)

            def one(t, carry):
                pltpu.make_async_remote_copy(
                    src_ref=zr.at[k, z], dst_ref=zr.at[k, z],
                    send_sem=zz_send.at[k], recv_sem=zz_recv.at[k],
                    device_id=at_plane((z + t) % planes), device_id_type=pl.DeviceIdType.MESH,
                ).start()
                return carry

            lax.fori_loop(1, planes, one, 0)

    def sum_planes(k):
        @pl.when(me < reducers)
        def _():
            wait_bytes(zr.at[k, pl.ds(0, planes - 1)], zz_recv.at[k])
            part = zr[k, 0].astype(jnp.float32)
            for n in range(1, planes):
                part = part + zr[k, n].astype(jnp.float32)
            ags[k] = (part * scale).astype(jnp.bfloat16)
            place = wg_out.at[k, pl.ds(pl.multiple_of(me * SLICE, 16), SLICE)]

            def one(t, carry):
                pltpu.make_async_remote_copy(
                    src_ref=ags.at[k], dst_ref=place,
                    send_sem=ag_send.at[k], recv_sem=ag_recv.at[k],
                    device_id=at((me + t) % group), device_id_type=pl.DeviceIdType.MESH,
                ).start()
                return carry

            lax.fori_loop(1, group, one, 0)
            pltpu.make_async_copy(ags.at[k], place, ag_recv.at[k]).start()

    conv(a0, cf, wv, 0, 32, forward(h0, h1, a1))
    conv(a1, cf, wv, 1, 96, forward(h1, h2, a2))
    conv(a2, cf, wv, 2, HALO, forward(h2, feat, None))
    send_out(feat, feat_out, 0)
    kernel_grad(2, a2, ct)
    wait_halo(ct, 1)
    conv(ct, cb, ft, 2, 128, backward(ct, h2, u2, r1))
    kernel_grad(1, a1, r1)
    sum_plane(2)
    conv(r1, cb, ft, 1, 192, backward(u2, h1, u1, r0))
    kernel_grad(0, a0, r0)
    sum_plane(1)
    sum_planes(2)
    conv(r0, cb, ft, 0, HALO, backward(u1, h0, None, grad))
    send_out(grad, grad_out, 1)
    sum_plane(0)
    sum_planes(1)
    sum_planes(0)

    wait_bytes(image.at[pl.ds(0, group - 1)], in_send.at[0])
    wait_bytes(image.at[pl.ds(0, group - 1)], in_send.at[1])
    for n in range(2):
        @pl.when(z < planes - 1)
        def _():
            wait_bytes(h0.at[:, pl.ds(0, HALO)], z_send.at[n, 0])

        @pl.when(z > 0)
        def _():
            wait_bytes(h0.at[:, pl.ds(0, HALO)], z_send.at[n, 1])

    wait_bytes(feat_out.at[pl.ds(0, group - 1)], out_send.at[0])
    wait_bytes(feat_out, out_recv.at[0])
    for k in range(3):
        @pl.when(me < reducers)
        def _():
            wait_bytes(rsb.at[k, pl.ds(0, (reducers - 1) * SLICE)], rs_send.at[k])
            wait_bytes(zr.at[k, pl.ds(0, planes - 1)], zz_send.at[k])
            wait_bytes(rsr.at[k, pl.ds(0, group - 1)], ag_send.at[k])

        @pl.when(me >= reducers)
        def _():
            wait_bytes(rsb.at[k], rs_send.at[k])

        wait_bytes(wg_out.at[k], ag_recv.at[k])
    wait_bytes(grad_out.at[pl.ds(0, group - 1)], out_send.at[1])
    wait_bytes(grad_out, out_recv.at[1])


def solution(mesh):
    nx, ny = mesh.shape["gx"], mesh.shape["gy"]
    planes = nx // SUB

    def shards(image, cotangent, weights):
        rows, cols, ch = image.shape
        width = SUB * cols
        total = width + 2 * HALO
        scale = 1.0 / math.sqrt(rows * ny * cols * nx)
        bf, f32 = jnp.bfloat16, jnp.float32
        dma = pltpu.SemaphoreType.DMA
        ext = pltpu.VMEM((ny, total, ch), bf)
        ext32 = pltpu.VMEM((ny, total, ch), f32)
        body = functools.partial(kernel, rows, cols, planes, scale)
        features, grad, wg = pl.pallas_call(
            body,
            out_shape=(
                jax.ShapeDtypeStruct(image.shape, bf),
                jax.ShapeDtypeStruct(image.shape, bf),
                jax.ShapeDtypeStruct((3, 9 * ch, ch), bf),
            ),
            in_specs=[pl.BlockSpec(memory_space=pl.ANY)] * 3,
            out_specs=[pl.BlockSpec(memory_space=pl.ANY)] * 3,
            scratch_shapes=[
                pltpu.VMEM((3, 3, 3, ch, ch), bf),
                pltpu.VMEM((3, 3, 3, ch, ch), bf),
                pltpu.VMEM((3, 6 * ch, 2 * ch), bf),
                pltpu.VMEM((3, 6 * ch, 2 * ch), bf),
                ext, ext, ext, ext, ext, ext, ext,
                ext32, ext, ext32, ext,
                pltpu.VMEM((ny, width, ch), bf),
                pltpu.VMEM((ny, width, ch), bf),
                pltpu.VMEM((3 * ch, 3 * ch), f32),
                pltpu.VMEM((3, 9 * ch, ch), bf),
                pltpu.VMEM((3, rows, SLICE, ch), bf),
                pltpu.VMEM((3, planes, SLICE, ch), bf),
                pltpu.VMEM((3, SLICE, ch), bf),
                dma,
                dma((2,)), dma((2,)), dma((2, 2)), dma((2, 2)), dma((2,)), dma((2,)),
                dma((3,)), dma((3,)), dma((3,)), dma((3,)), dma((3,)), dma((3,)),
            ],
            compiler_params=pltpu.CompilerParams(
                collective_id=0, has_side_effects=True, vmem_limit_bytes=56 * 1024 * 1024
            ),
        )(image, cotangent, weights)
        return features, grad, wg.reshape(3, 3, 3, ch, ch).astype(f32)

    return jax.shard_map(
        shards,
        mesh=mesh,
        in_specs=(P("gy", "gx", None), P("gy", "gx", None), P()),
        out_specs=(P("gy", "gx", None), P("gy", "gx", None), P()),
        check_vma=False,
    )
```

time: 677 us -> 86.1 us (0.13); the launches traced: 667 us -> 86 us
  waiting for transfers between devices: 460 us -> 0 us
  local copies, waits for them, and re-layouts: 86.5 us -> 1.59 us
  Pallas kernels: 0 us -> 81.1 us
  starting transfers between devices: 61.5 us -> 0 us
  matrix products: 29.7 us -> 0 us
  between operations: 15.3 us -> 0.66 us
  other arithmetic: 13 us -> 2.67 us
    psum x1 -> x0, waiting for transfers between devices: 256 us -> none  [shards(): stacked = lax.psum(stacked, ('gx', 'gy'))]
    ppermute x24 -> x0, waiting for transfers between devices: 205 us -> none  [the longest x16 201 us: from_behind(): return lax.ppermute(block, axis, route)]
    pallas_call x0 -> x1, Pallas kernels: none -> 81.1 us  [shards(): pl.pallas_call(body, out_shape=(jax.ShapeDtypeStruct(image.shape, bf), ja...]
    ppermute x24 -> x0, starting transfers between devices: 61.5 us -> none  [the longest x16 38 us: from_behind(): return lax.ppermute(block, axis, route)]
    another operation x7 -> x0, local copies, waits for them, and re-layouts: 53.1 us -> none  [gather_taps(): jnp.stack(tap_list, axis=2).reshape(row_count * col_count, 9 * channels)]
    dot_general x9 -> x0, matrix products: 29.7 us -> none  [the longest x3 12.8 us: shards(): lax.dot_general(patch_list[k], rounded.reshape(row_count * col_count, cha...]
    unnamed x76 -> x6, local copies, waits for them, and re-layouts: 25.7 us -> 1.59 us
  transfers between devices with their start and end apart: 25 -> 0, of which waited for: 11 -> 0; matrix products, arithmetic and copies ran while one was open for 17% -> 0% of each run, Pallas kernels for 0% -> 0%
where the time goes in v1:
time: 86.1 us; the launch traced here: 86 us
  Pallas kernels  81.1 us (94%)
  other arithmetic  2.67 us (3%)
  local copies, waits for them, and re-layouts  1.59 us (2%)
    pallas_call x1, Pallas kernels, shards(): pl.pallas_call(body, out_shape=(jax.ShapeDtypeStruct(image.shape, bf), ja...  81.1 us
    convert_element_type x1, other arithmetic, shards(): return (features, grad, wg.reshape(3, 3, 3, ch, ch).astype(f32))  2.67 us

profile of v1, /device:TPU:1, one launch (start us, length us, event | category | flops | bytes accessed | tf_op | source)
XLA Modules:
  0.0 86.0 jit_solution(15862860960964158819)
XLA Ops:
  0.6 81.1 %shard_map.58 = (bf16[32,64,128]{2,1,0:T(8,128)(2,1)}, bf16[32,64,128]{2,1,0:T(8,128)(2,1)}, bf16[3,1152,128]{2,1,0:T(8,128)(2,1)}) custom-call(bf16[32,64,128]{2,1,0:T(8,128)(2,1)} %image.1, bf16[32,64,128]{2,1,0:T(8,128)(2,1)} %cotangent.1, bf16[3,3,3,128,128]{4,3,2,1,0:T(8,128)(2,1)} %weights.1), custom_call_target="tpu_custom_call" | custom-call | tf_op jit(solution)/shard_map/pallas_call | solution.py:385
  81.7 0.0 copy-start.1
  81.7 0.0 copy-start
  81.7 2.7 %convert.1 = f32[3,3,3,128,128]{4,3,2,1,0:T(8,128)} convert(bf16[3,3,3,128,128]{4,3,2,1,0:T(8,128)(2,1)} %bitcast.2) | non-fusion elementwise | flops 442368 | bytes 2654208 | tf_op jit(solution)/shard_map/convert_element_type | solution.py:416
  84.4 0.0 copy-done.1
  84.4 0.8 copy.8
  85.2 0.0 copy-done
  85.2 0.8 copy.9
Async XLA Ops:
  81.7 2.7 %copy-start.1 = (bf16[32,64,128]{2,1,0:T(8,128)(2,1)S(1)}, bf16[32,64,128]{2,1,0:T(8,128)(2,1)}, u32[]{:S(2)}) copy-start(bf16[32,64,128]{2,1,0:T(8,128)(2,1)} %get-tuple-element.12) | copy-start | bytes 1572868
  81.7 3.5 %copy-start = (bf16[32,64,128]{2,1,0:T(8,128)(2,1)S(1)}, bf16[32,64,128]{2,1,0:T(8,128)(2,1)}, u32[]{:S(2)}) copy-start(bf16[32,64,128]{2,1,0:T(8,128)(2,1)} %get-tuple-element.13) | copy-start | bytes 1572868

commit v2 on v1

--- a/solution.py
+++ b/solution.py
@@ -11,7 +11,9 @@
 SUB = 4
 HALO = 224
 STEPS = (1, 2, 4)
-SLICE = 48
+PIECES = ((0, 128), (128, 64), (192, 32))
+SLICE, SLICES = 48, 12
+HALF = SLICE * SLICES
 
 
 def pairs_of(step):
@@ -34,13 +36,14 @@
     wv, ft, cf, cb,
     h0, a0, h1, a1, h2, a2, ct,
     u2, r1, u1, r0, feat, grad,
-    wacc, rsb, rsr, zr, ags,
+    wacc, psb, prv, rsb, rsr, zr, wg,
     w_sem, in_send, in_recv, z_send, z_recv, out_send, out_recv,
-    rs_send, rs_recv, zz_send, zz_recv, ag_send, ag_recv,
+    pp_send, pp_recv, rs_send, rs_recv, zz_send, zz_recv, ag_send, ag_recv, pa_send, pa_recv,
 ):
     gx, gy = lax.axis_index("gx"), lax.axis_index("gy")
     z, c = gx // SUB, gx % SUB
     me = gy * SUB + c
+    core = c % 2
     group = rows
     width = SUB * cols
     own = pl.ds(HALO, width)
@@ -72,23 +75,25 @@
 
     def send_in(source, ext, n):
         place = ext.at[gy, pl.ds(pl.multiple_of(HALO + c * cols, 32), cols)]
-
-        def one(t, carry):
-            q = (me + t) % group
+        for s in range(8):
+            g = lax.rem(gy + (8 - s), 8)
+            for m in range(SUB):
+                cc = lax.rem(c + m, SUB)
+                if s == 0 and m == 0:
+                    pltpu.make_async_copy(source.at[me], place, in_recv.at[n, gy]).start()
+                else:
+                    pltpu.make_async_remote_copy(
+                        src_ref=source.at[g * SUB + cc], dst_ref=place,
+                        send_sem=in_send.at[n], recv_sem=in_recv.at[n, gy],
+                        device_id={"gx": z * SUB + cc, "gy": g}, device_id_type=pl.DeviceIdType.MESH,
+                    ).start()
+
+    def send_halo(ext, row, near, size, n):
+        @pl.when(z < planes - 1)
+        def _():
             pltpu.make_async_remote_copy(
-                src_ref=source.at[q], dst_ref=place, send_sem=in_send.at[n], recv_sem=in_recv.at[n],
-                device_id=at(q), device_id_type=pl.DeviceIdType.MESH,
-            ).start()
-            return carry
-
-        lax.fori_loop(1, group, one, 0)
-        pltpu.make_async_copy(source.at[me], place, in_recv.at[n]).start()
-
-    def send_halo(ext, n):
-        @pl.when(z < planes - 1)
-        def _():
-            pltpu.make_async_remote_copy(
-                src_ref=ext.at[:, pl.ds(width, HALO)], dst_ref=ext.at[:, pl.ds(0, HALO)],
+                src_ref=ext.at[row, pl.ds(HALO + width - near - size, size)],
+                dst_ref=ext.at[row, pl.ds(HALO - near - size, size)],
                 send_sem=z_send.at[n, 0], recv_sem=z_recv.at[n, 0],
                 device_id=at_plane(z + 1), device_id_type=pl.DeviceIdType.MESH,
             ).start()
@@ -96,19 +101,20 @@
         @pl.when(z > 0)
         def _():
             pltpu.make_async_remote_copy(
-                src_ref=ext.at[:, pl.ds(HALO, HALO)], dst_ref=ext.at[:, pl.ds(HALO + width, HALO)],
+                src_ref=ext.at[row, pl.ds(HALO + near, size)],
+                dst_ref=ext.at[row, pl.ds(HALO + width + near, size)],
                 send_sem=z_send.at[n, 1], recv_sem=z_recv.at[n, 1],
                 device_id=at_plane(z - 1), device_id_type=pl.DeviceIdType.MESH,
             ).start()
 
-    def wait_halo(ext, n):
+    def wait_halo(ext, near, size, n):
         @pl.when(z > 0)
         def _():
-            wait_bytes(ext.at[:, pl.ds(0, HALO)], z_recv.at[n, 0])
+            wait_bytes(ext.at[:, pl.ds(HALO - near - size, size)], z_recv.at[n, 0])
 
         @pl.when(z < planes - 1)
         def _():
-            wait_bytes(ext.at[:, pl.ds(HALO + width, HALO)], z_recv.at[n, 1])
+            wait_bytes(ext.at[:, pl.ds(HALO + width + near, size)], z_recv.at[n, 1])
 
     def zero_edges(ext):
         @pl.when(z == 0)
@@ -134,20 +140,11 @@
             block.at[gy, pl.ds(pl.multiple_of(c * cols, 32), cols)], out.at[me], out_recv.at[n]
         ).start()
 
-    send_in(image, h0, 0)
-    zero_edges(h0)
-    zero_edges(ct)
-
-    w_copy.wait()
-
-    def flip(n, carry):
-        k, m = n // 9, n % 9
-        i, j = m // 3, m % 3
+    def flip(n):
+        k, i, j = n // 9, n // 3 % 3, n % 3
         ft[k, i, j] = wv[k, 2 - i, 2 - j].astype(jnp.float32).T.astype(jnp.bfloat16)
-        return carry
-
-    lax.fori_loop(0, 27, flip, 0)
-    for src, dst in ((wv, cf), (ft, cb)):
+
+    def two_rows(src, dst):
         for k in range(3):
             for j in range(3):
                 base = j * 256
@@ -156,14 +153,26 @@
                 dst[k, base + 128 : base + 256, 0:128] = src[k, 2, j]
                 dst[k, base + 128 : base + 256, 128:256] = src[k, 1, j]
 
-    wait_bytes(h0.at[:, own], in_recv.at[0])
-    send_halo(h0, 0)
+    send_in(image, h0, 0)
     send_in(cotangent, ct, 1)
-    for a in range(8):
+    zero_edges(h0)
+    w_copy.wait()
+    two_rows(wv, cf)
+    for s in range(8):
+        for n in range(4 * s, min(4 * s + 4, 27)):
+            flip(n)
+        a = lax.rem(gy + s, 8)
+        wait_bytes(h0.at[a, own], in_recv.at[0, a])
+        send_halo(h0, a, 0, HALO, 0)
         a0[a, HALO : HALO + width, :] = elu(h0[a, HALO : HALO + width, :])
-    wait_bytes(ct.at[:, own], in_recv.at[1])
-    send_halo(ct, 1)
-    wait_halo(h0, 0)
+    for s in range(8):
+        a = lax.rem(gy + s, 8)
+        wait_bytes(ct.at[a, own], in_recv.at[1, a])
+        send_halo(ct, a, *PIECES[0], 1)
+    for n in (1, 2):
+        send_halo(ct, pl.ds(0, 8), *PIECES[n], n + 1)
+    zero_edges(ct)
+    wait_halo(h0, 0, HALO, 0)
     for a in range(8):
         a0[a, 0:HALO, :] = elu(h0[a, 0:HALO, :])
         a0[a, HALO + width :, :] = elu(h0[a, HALO + width :, :])
@@ -171,32 +180,64 @@
     left_in = z > 0
     right_in = z < planes - 1
 
-    def conv(src, both, single, k, lo, emit):
+    def sides(near, size):
+        return [(HALO - near - size, size, left_in), (HALO + width + near, size, right_in)]
+
+    centre = [(HALO, width, None)]
+
+    def conv(src, both, single, k, segments, merge, emit):
         step, d = STEPS[k], 32 * STEPS[k]
-        chunks = [(HALO, width, None)]
-        if lo < HALO:
-            chunks = [(lo, HALO - lo, left_in), chunks[0], (HALO + width, HALO - lo, right_in)]
-        for start, size, inside in chunks:
-            def taps(which):
+
+        def taps(rows_of, blocks):
+            out = []
+            for block in blocks:
+                start, size, _ = block[2]
                 parts = []
                 for j in range(3):
                     at_col = start + (j - 1) * d
-                    parts += [src[r, at_col : at_col + size, :] for r in which]
-                return jnp.concatenate(parts, axis=1)
-
-            for first, second in pairs_of(step):
-                acc = jnp.dot(taps((first, second)), both[k], preferred_element_type=jnp.float32)
-                one, two = acc[:, 0:128], acc[:, 128:256]
-                if first - step >= 0:
-                    one = one + jnp.dot(
-                        taps((first - step,)), single[k, 0].reshape(384, 128), preferred_element_type=jnp.float32
-                    )
-                if second + step < 8:
-                    two = two + jnp.dot(
-                        taps((second + step,)), single[k, 2].reshape(384, 128), preferred_element_type=jnp.float32
-                    )
-                emit(first, start, size, inside, one)
-                emit(second, start, size, inside, two)
+                    parts += [src[r, at_col : at_col + size, :] for r in rows_of(block)]
+                out.append(jnp.concatenate(parts, axis=1))
+            return out[0] if len(out) == 1 else jnp.concatenate(out, axis=0)
+
+        def key(block):
+            return block[0], block[2][0]
+
+        def cut(value, blocks):
+            pieces, at_row = {}, 0
+            for block in blocks:
+                size = block[2][1]
+                pieces[key(block)] = value[at_row : at_row + size]
+                at_row += size
+            return pieces
+
+        pairs = pairs_of(step)
+        for group in [pairs] if merge else [[p] for p in pairs]:
+            blocks = [(f, g, seg) for f, g in group for seg in segments]
+            acc = jnp.dot(taps(lambda b: (b[0], b[1]), blocks), both[k], preferred_element_type=jnp.float32)
+            first, second = cut(acc[:, 0:128], blocks), cut(acc[:, 128:256], blocks)
+            above = [b for b in blocks if b[0] - step >= 0]
+            below = [b for b in blocks if b[1] + step < 8]
+            up, down = {}, {}
+            if above:
+                up = cut(
+                    jnp.dot(
+                        taps(lambda b: (b[0] - step,), above), single[k, 0].reshape(384, 128),
+                        preferred_element_type=jnp.float32,
+                    ),
+                    above,
+                )
+            if below:
+                down = cut(
+                    jnp.dot(
+                        taps(lambda b: (b[1] + step,), below), single[k, 2].reshape(384, 128),
+                        preferred_element_type=jnp.float32,
+                    ),
+                    below,
+                )
+            for b in blocks:
+                n = key(b)
+                emit(b[0], *b[2], first[n] + up[n] if n in up else first[n])
+                emit(b[1], *b[2], second[n] + down[n] if n in down else second[n])
 
     def forward(old, new, active):
         def emit(row, start, size, inside, value):
@@ -253,39 +294,47 @@
             )
         for i in range(3):
             for j in range(3):
-                rsb[k, (i * 3 + j) * 128 : (i * 3 + j + 1) * 128, :] = wacc[
+                psb[k, (i * 3 + j) * 128 : (i * 3 + j + 1) * 128, :] = wacc[
                     j * 128 : (j + 1) * 128, i * 128 : (i + 1) * 128
-                ].astype(jnp.bfloat16)
-
-        def one(t, carry):
-            q = (me + t) % group
-
-            @pl.when(q < reducers)
-            def _():
+                ]
+        pltpu.make_async_remote_copy(
+            src_ref=psb.at[k, pl.ds(pl.multiple_of((1 - core) * HALF, 16), HALF)], dst_ref=prv.at[k],
+            send_sem=pp_send.at[k], recv_sem=pp_recv.at[k],
+            device_id={"gx": gx + 1 - 2 * core, "gy": gy}, device_id_type=pl.DeviceIdType.MESH,
+        ).start()
+
+    def sum_pair(k):
+        wait_bytes(prv.at[k], pp_recv.at[k])
+        rsb[k] = (psb[k, pl.ds(pl.multiple_of(core * HALF, 16), HALF)] + prv[k]).astype(jnp.bfloat16)
+        start = lax.rem(me // 2, SLICES)
+        for t in range(SLICES):
+            n = lax.rem(start + t, SLICES)
+            part = rsb.at[k, pl.ds(pl.multiple_of(n * SLICE, 16), SLICE)]
+            place = rsr.at[k, me // 2]
+
+            def send():
                 pltpu.make_async_remote_copy(
-                    src_ref=rsb.at[k, pl.ds(pl.multiple_of(q * SLICE, 16), SLICE)], dst_ref=rsr.at[k, me],
-                    send_sem=rs_send.at[k], recv_sem=rs_recv.at[k],
-                    device_id=at(q), device_id_type=pl.DeviceIdType.MESH,
+                    src_ref=part, dst_ref=place, send_sem=rs_send.at[k], recv_sem=rs_recv.at[k],
+                    device_id=at(2 * n + core), device_id_type=pl.DeviceIdType.MESH,
                 ).start()
 
-            return carry
-
-        lax.fori_loop(1, group, one, 0)
-
-        @pl.when(me < reducers)
-        def _():
-            pltpu.make_async_copy(
-                rsb.at[k, pl.ds(pl.multiple_of(me * SLICE, 16), SLICE)], rsr.at[k, me], rs_recv.at[k]
-            ).start()
-
-    reducers = 9 * 128 // SLICE
+            if t > 0:
+                send()
+            else:
+                pl.when(me >= reducers)(send)
+
+                @pl.when(me < reducers)
+                def _():
+                    pltpu.make_async_copy(part, place, rs_recv.at[k]).start()
+
+    reducers = 2 * SLICES
 
     def sum_plane(k):
         @pl.when(me < reducers)
         def _():
             wait_bytes(rsr.at[k], rs_recv.at[k])
             part = rsr[k, 0].astype(jnp.float32)
-            for n in range(1, group):
+            for n in range(1, group // 2):
                 part = part + rsr[k, n].astype(jnp.float32)
             zr[k, z] = part.astype(jnp.bfloat16)
 
@@ -306,66 +355,115 @@
             part = zr[k, 0].astype(jnp.float32)
             for n in range(1, planes):
                 part = part + zr[k, n].astype(jnp.float32)
-            ags[k] = (part * scale).astype(jnp.bfloat16)
-            place = wg_out.at[k, pl.ds(pl.multiple_of(me * SLICE, 16), SLICE)]
-
-            def one(t, carry):
+            place = wg.at[k, pl.ds(pl.multiple_of(core * HALF + me // 2 * SLICE, 16), SLICE)]
+            place[...] = (part * scale).astype(jnp.bfloat16)
+            for t in range(1, group // 2):
                 pltpu.make_async_remote_copy(
-                    src_ref=ags.at[k], dst_ref=place,
-                    send_sem=ag_send.at[k], recv_sem=ag_recv.at[k],
-                    device_id=at((me + t) % group), device_id_type=pl.DeviceIdType.MESH,
+                    src_ref=place, dst_ref=place, send_sem=ag_send.at[k], recv_sem=ag_recv.at[k],
+                    device_id=at(lax.rem(me + 2 * t, group)), device_id_type=pl.DeviceIdType.MESH,
                 ).start()
-                return carry
-
-            lax.fori_loop(1, group, one, 0)
-            pltpu.make_async_copy(ags.at[k], place, ag_recv.at[k]).start()
-
-    conv(a0, cf, wv, 0, 32, forward(h0, h1, a1))
-    conv(a1, cf, wv, 1, 96, forward(h1, h2, a2))
-    conv(a2, cf, wv, 2, HALO, forward(h2, feat, None))
+
+    def gather_pair(k):
+        for here, count in ((me < reducers, SLICES - 1), (me >= reducers, SLICES)):
+            @pl.when(here)
+            def _():
+                wait_bytes(wg.at[k, pl.ds(0, count * SLICE)], ag_recv.at[k])
+
+        part = wg.at[k, pl.ds(pl.multiple_of(core * HALF, 16), HALF)]
+        pltpu.make_async_remote_copy(
+            src_ref=part, dst_ref=part, send_sem=pa_send.at[k], recv_sem=pa_recv.at[k],
+            device_id={"gx": gx + 1 - 2 * core, "gy": gy}, device_id_type=pl.DeviceIdType.MESH,
+        ).start()
+
+    def store_grad(k):
+        wait_bytes(wg.at[k, pl.ds(0, HALF)], pa_recv.at[k])
+        pltpu.make_async_copy(wg.at[k], wg_out.at[k], w_sem).start()
+
+    conv(a0, cf, wv, 0, centre, False, forward(h0, h1, a1))
+    conv(a0, cf, wv, 0, sides(0, 192), False, forward(h0, h1, a1))
+    conv(a1, cf, wv, 1, centre, False, forward(h1, h2, a2))
+    conv(a1, cf, wv, 1, sides(0, 128), False, forward(h1, h2, a2))
+    conv(a2, cf, wv, 2, centre, False, forward(h2, feat, None))
+    kernel_grad(2, a2, ct)
+    two_rows(ft, cb)
+    sum_pair(2)
     send_out(feat, feat_out, 0)
-    kernel_grad(2, a2, ct)
-    wait_halo(ct, 1)
-    conv(ct, cb, ft, 2, 128, backward(ct, h2, u2, r1))
+    back2, back1 = backward(ct, h2, u2, r1), backward(u2, h1, u1, r0)
+    wait_halo(ct, *PIECES[0], 1)
+    conv(ct, cb, ft, 2, centre, False, back2)
     kernel_grad(1, a1, r1)
+    wait_halo(ct, *PIECES[1], 2)
+    conv(ct, cb, ft, 2, sides(0, 64), True, back2)
+    sum_pair(1)
+    conv(r1, cb, ft, 1, centre, False, back1)
+    kernel_grad(0, a0, r0)
+    wait_halo(ct, *PIECES[2], 3)
+    conv(ct, cb, ft, 2, sides(64, 32), True, back2)
+    sum_pair(0)
+    conv(r1, cb, ft, 1, sides(0, 32), True, back1)
+    conv(r0, cb, ft, 0, centre, False, backward(u1, h0, None, grad))
+    send_out(grad, grad_out, 1)
     sum_plane(2)
-    conv(r1, cb, ft, 1, 192, backward(u2, h1, u1, r0))
-    kernel_grad(0, a0, r0)
     sum_plane(1)
+    sum_plane(0)
     sum_planes(2)
-    conv(r0, cb, ft, 0, HALO, backward(u1, h0, None, grad))
-    send_out(grad, grad_out, 1)
-    sum_plane(0)
     sum_planes(1)
     sum_planes(0)
+    gather_pair(2)
+    gather_pair(1)
+    gather_pair(0)
+    store_grad(2)
+    store_grad(1)
+    store_grad(0)
 
     wait_bytes(image.at[pl.ds(0, group - 1)], in_send.at[0])
     wait_bytes(image.at[pl.ds(0, group - 1)], in_send.at[1])
-    for n in range(2):
+    for n, size in enumerate((HALO, 128, 64, 32)):
         @pl.when(z < planes - 1)
         def _():
-            wait_bytes(h0.at[:, pl.ds(0, HALO)], z_send.at[n, 0])
+            wait_bytes(h0.at[:, pl.ds(0, size)], z_send.at[n, 0])
 
         @pl.when(z > 0)
         def _():
-            wait_bytes(h0.at[:, pl.ds(0, HALO)], z_send.at[n, 1])
+            wait_bytes(h0.at[:, pl.ds(0, size)], z_send.at[n, 1])
 
     wait_bytes(feat_out.at[pl.ds(0, group - 1)], out_send.at[0])
     wait_bytes(feat_out, out_recv.at[0])
     for k in range(3):
         @pl.when(me < reducers)
         def _():
-            wait_bytes(rsb.at[k, pl.ds(0, (reducers - 1) * SLICE)], rs_send.at[k])
+            wait_bytes(rsb.at[k, pl.ds(0, HALF - SLICE)], rs_send.at[k])
             wait_bytes(zr.at[k, pl.ds(0, planes - 1)], zz_send.at[k])
-            wait_bytes(rsr.at[k, pl.ds(0, group - 1)], ag_send.at[k])
+            wait_bytes(feat_out.at[pl.ds(0, group // 2 - 1), pl.ds(0, SLICE)], ag_send.at[k])
 
         @pl.when(me >= reducers)
         def _():
             wait_bytes(rsb.at[k], rs_send.at[k])
 
-        wait_bytes(wg_out.at[k], ag_recv.at[k])
+        wait_bytes(psb.at[k, pl.ds(0, HALF)], pp_send.at[k])
+        wait_bytes(wg.at[k, pl.ds(0, HALF)], pa_send.at[k])
+    wait_bytes(wg, w_sem)
     wait_bytes(grad_out.at[pl.ds(0, group - 1)], out_send.at[1])
     wait_bytes(grad_out, out_recv.at[1])
+
+
+def finish(feat_in, grad_in, wg_in, feat_out, grad_out, wg_out, feat, grad, narrow, wide, sems):
+    sources = [feat_in, grad_in] + [wg_in.at[k] for k in range(3)]
+    places = [feat, grad] + [narrow.at[k] for k in range(3)]
+    loads = [pltpu.make_async_copy(a, b, sems.at[n]) for n, (a, b) in enumerate(zip(sources, places))]
+    sources = [feat, grad] + [wide.at[k] for k in range(3)]
+    places = [feat_out, grad_out] + [wg_out.at[k] for k in range(3)]
+    stores = [pltpu.make_async_copy(a, b, sems.at[5 + n]) for n, (a, b) in enumerate(zip(sources, places))]
+    order = (2, 3, 4, 0, 1)
+    for n in order:
+        loads[n].start()
+    for n in order:
+        loads[n].wait()
+        if n >= 2:
+            wide[n - 2] = narrow[n - 2].astype(jnp.float32)
+        stores[n].start()
+    for copy in stores:
+        copy.wait()
 
 
 def solution(mesh):
@@ -401,19 +499,39 @@
                 pltpu.VMEM((ny, width, ch), bf),
                 pltpu.VMEM((ny, width, ch), bf),
                 pltpu.VMEM((3 * ch, 3 * ch), f32),
-                pltpu.VMEM((3, 9 * ch, ch), bf),
-                pltpu.VMEM((3, rows, SLICE, ch), bf),
+                pltpu.VMEM((3, 2 * HALF, ch), f32),
+                pltpu.VMEM((3, HALF, ch), f32),
+                pltpu.VMEM((3, HALF, ch), bf),
+                pltpu.VMEM((3, rows // 2, SLICE, ch), bf),
                 pltpu.VMEM((3, planes, SLICE, ch), bf),
-                pltpu.VMEM((3, SLICE, ch), bf),
+                pltpu.VMEM((3, 2 * HALF, ch), bf),
                 dma,
-                dma((2,)), dma((2,)), dma((2, 2)), dma((2, 2)), dma((2,)), dma((2,)),
-                dma((3,)), dma((3,)), dma((3,)), dma((3,)), dma((3,)), dma((3,)),
+                dma((2,)), dma((2, ny)), dma((4, 2)), dma((4, 2)), dma((2,)), dma((2,)),
+                *[dma((3,))] * 10,
             ],
             compiler_params=pltpu.CompilerParams(
                 collective_id=0, has_side_effects=True, vmem_limit_bytes=56 * 1024 * 1024
             ),
         )(image, cotangent, weights)
-        return features, grad, wg.reshape(3, 3, 3, ch, ch).astype(f32)
+        features, grad, wg = pl.pallas_call(
+            finish,
+            out_shape=(
+                jax.ShapeDtypeStruct(image.shape, bf),
+                jax.ShapeDtypeStruct(image.shape, bf),
+                jax.ShapeDtypeStruct((3, 9 * ch, ch), f32),
+            ),
+            in_specs=[pl.BlockSpec(memory_space=pl.ANY)] * 3,
+            out_specs=[pl.BlockSpec(memory_space=pl.ANY)] * 3,
+            scratch_shapes=[
+                pltpu.VMEM(image.shape, bf),
+                pltpu.VMEM(image.shape, bf),
+                pltpu.VMEM((3, 9 * ch, ch), bf),
+                pltpu.VMEM((3, 9 * ch, ch), f32),
+                dma((10,)),
+            ],
+            compiler_params=pltpu.CompilerParams(vmem_limit_bytes=56 * 1024 * 1024),
+        )(features, grad, wg)
+        return features, grad, wg.reshape(3, 3, 3, ch, ch)
 
     return jax.shard_map(
         shards,

time: 86.1 us -> 72.1 us (0.84)
  Pallas kernels: 81.1 us -> 71.4 us
  other arithmetic: 2.67 us -> 0 us
  local copies, waits for them, and re-layouts: 1.59 us -> 0 us
    pallas_call x1, Pallas kernels: 81.1 us -> 68.7 us  [shards(): pl.pallas_call(body, out_shape=(jax.ShapeDtypeStruct(image.shape, bf), ja...]
    convert_element_type x1 -> x0, other arithmetic: 2.67 us -> none  [shards(): return (features, grad, wg.reshape(3, 3, 3, ch, ch).astype(f32))]
    pallas_call x0 -> x1, Pallas kernels: none -> 2.64 us  [shards(): pl.pallas_call(finish, out_shape=(jax.ShapeDtypeStruct(image.shape, bf),...]
    unnamed x6 -> x0, local copies, waits for them, and re-layouts: 1.59 us -> none
where the time goes in v2:
time: 72.1 us; the launch traced here: 72 us
  Pallas kernels  71.4 us (99%)
    pallas_call x1, Pallas kernels, shards(): pl.pallas_call(body, out_shape=(jax.ShapeDtypeStruct(image.shape, bf), ja...  68.7 us
    pallas_call x1, Pallas kernels, shards(): pl.pallas_call(finish, out_shape=(jax.ShapeDtypeStruct(image.shape, bf),...  2.64 us

profile of v2, /device:TPU:1, one launch (start us, length us, event | category | flops | bytes accessed | tf_op | source)
XLA Modules:
  0.0 72.0 jit_solution(7066372148428249345)
XLA Ops:
  0.6 68.7 %shard_map.58 = (bf16[32,64,128]{2,1,0:T(8,128)(2,1)}, bf16[32,64,128]{2,1,0:T(8,128)(2,1)}, bf16[3,1152,128]{2,1,0:T(8,128)(2,1)}) custom-call(bf16[32,64,128]{2,1,0:T(8,128)(2,1)} %image.1, bf16[32,64,128]{2,1,0:T(8,128)(2,1)} %cotangent.1, bf16[3,3,3,128,128]{4,3,2,1,0:T(8,128)(2,1)} %weights.1), custom_call_target="tpu_custom_call" | custom-call | tf_op jit(solution)/shard_map/pallas_call | solution.py:483
  69.4 2.6 %shard_map.59 = (bf16[32,64,128]{2,1,0:T(8,128)(2,1)}, bf16[32,64,128]{2,1,0:T(8,128)(2,1)}, f32[3,1152,128]{2,1,0:T(8,128)}) custom-call(bf16[32,64,128]{2,1,0:T(8,128)(2,1)} %get-tuple-element.9.feat_in, bf16[32,64,128]{2,1,0:T(8,128)(2,1)} %get-tuple-element.10.grad_in, bf16[3,1152,128]{2,1,0:T(8,128)(2,1)} %get-tuple-element.11.wg_in), custom_call_target="tpu_custom_call" | custom-call | tf_op jit(solution)/shard_map/pallas_call | solution.py:516

commit v3 on v2

--- a/solution.py
+++ b/solution.py
@@ -41,17 +41,15 @@
     pp_send, pp_recv, rs_send, rs_recv, zz_send, zz_recv, ag_send, ag_recv, pa_send, pa_recv,
 ):
     gx, gy = lax.axis_index("gx"), lax.axis_index("gy")
-    z, c = gx // SUB, gx % SUB
+    z, c = lax.div(gx, SUB), lax.rem(gx, SUB)
     me = gy * SUB + c
-    core = c % 2
+    core, y_lo = lax.rem(c, 2), lax.div(c, 2)
+    pair = gy * 2 + y_lo
     group = rows
     width = SUB * cols
     own = pl.ds(HALO, width)
     total = width + 2 * HALO
 
-    def at(q):
-        return {"gx": z * SUB + q % SUB, "gy": q // SUB}
-
     def at_plane(p):
         return {"gx": p * SUB + c, "gy": gy}
 
@@ -60,17 +58,18 @@
 
     barrier = pltpu.get_barrier_semaphore()
 
-    def greet(t, carry):
-        pl.semaphore_signal(barrier, inc=1, device_id=at((me + t) % group), device_id_type=pl.DeviceIdType.MESH)
-        return carry
-
-    lax.fori_loop(1, group, greet, 0)
-
-    def greet_plane(t, carry):
-        pl.semaphore_signal(barrier, inc=1, device_id=at_plane((z + t) % planes), device_id_type=pl.DeviceIdType.MESH)
-        return carry
-
-    lax.fori_loop(1, planes, greet_plane, 0)
+    for p in range(1, planes):
+        pl.semaphore_signal(
+            barrier, inc=1, device_id=at_plane(lax.rem(z + p, planes)), device_id_type=pl.DeviceIdType.MESH
+        )
+    for s in reversed(range(8)):
+        g = lax.rem(gy + s, 8)
+        for m in range(SUB):
+            if s or m:
+                pl.semaphore_signal(
+                    barrier, inc=1, device_id={"gx": z * SUB + lax.rem(c + m, SUB), "gy": g},
+                    device_id_type=pl.DeviceIdType.MESH,
+                )
     pl.semaphore_wait(barrier, group - 1 + planes - 1)
 
     def send_in(source, ext, n):
@@ -126,19 +125,19 @@
             ext[:, HALO + width :, :] = jnp.zeros((8, HALO, 128), ext.dtype)
 
     def send_out(block, out, n):
-        def one(t, carry):
-            q = (me + t) % group
-            pltpu.make_async_remote_copy(
-                src_ref=block.at[q // SUB, pl.ds(pl.multiple_of((q % SUB) * cols, 32), cols)], dst_ref=out.at[me],
-                send_sem=out_send.at[n], recv_sem=out_recv.at[n],
-                device_id=at(q), device_id_type=pl.DeviceIdType.MESH,
-            ).start()
-            return carry
-
-        lax.fori_loop(1, group, one, 0)
-        pltpu.make_async_copy(
-            block.at[gy, pl.ds(pl.multiple_of(c * cols, 32), cols)], out.at[me], out_recv.at[n]
-        ).start()
+        place = out.at[me]
+        for s in range(8):
+            g = lax.rem(gy + s, 8)
+            for m in range(SUB):
+                cc = lax.rem(c + m, SUB)
+                part = block.at[g, pl.ds(pl.multiple_of(cc * cols, 32), cols)]
+                if s == 0 and m == 0:
+                    pltpu.make_async_copy(part, place, out_recv.at[n]).start()
+                else:
+                    pltpu.make_async_remote_copy(
+                        src_ref=part, dst_ref=place, send_sem=out_send.at[n], recv_sem=out_recv.at[n],
+                        device_id={"gx": z * SUB + cc, "gy": g}, device_id_type=pl.DeviceIdType.MESH,
+                    ).start()
 
     def flip(n):
         k, i, j = n // 9, n // 3 % 3, n % 3
@@ -306,16 +305,17 @@
     def sum_pair(k):
         wait_bytes(prv.at[k], pp_recv.at[k])
         rsb[k] = (psb[k, pl.ds(pl.multiple_of(core * HALF, 16), HALF)] + prv[k]).astype(jnp.bfloat16)
-        start = lax.rem(me // 2, SLICES)
+        start = lax.rem(pair, SLICES)
         for t in range(SLICES):
             n = lax.rem(start + t, SLICES)
             part = rsb.at[k, pl.ds(pl.multiple_of(n * SLICE, 16), SLICE)]
-            place = rsr.at[k, me // 2]
+            place = rsr.at[k, pair]
 
             def send():
                 pltpu.make_async_remote_copy(
                     src_ref=part, dst_ref=place, send_sem=rs_send.at[k], recv_sem=rs_recv.at[k],
-                    device_id=at(2 * n + core), device_id_type=pl.DeviceIdType.MESH,
+                    device_id={"gx": z * SUB + lax.rem(n, 2) * 2 + core, "gy": lax.div(n, 2)},
+                    device_id_type=pl.DeviceIdType.MESH,
                 ).start()
 
             if t > 0:
@@ -338,15 +338,12 @@
                 part = part + rsr[k, n].astype(jnp.float32)
             zr[k, z] = part.astype(jnp.bfloat16)
 
-            def one(t, carry):
+            for p in range(1, planes):
                 pltpu.make_async_remote_copy(
                     src_ref=zr.at[k, z], dst_ref=zr.at[k, z],
                     send_sem=zz_send.at[k], recv_sem=zz_recv.at[k],
-                    device_id=at_plane((z + t) % planes), device_id_type=pl.DeviceIdType.MESH,
+                    device_id=at_plane(lax.rem(z + p, planes)), device_id_type=pl.DeviceIdType.MESH,
                 ).start()
-                return carry
-
-            lax.fori_loop(1, planes, one, 0)
 
     def sum_planes(k):
         @pl.when(me < reducers)
@@ -355,13 +352,17 @@
             part = zr[k, 0].astype(jnp.float32)
             for n in range(1, planes):
                 part = part + zr[k, n].astype(jnp.float32)
-            place = wg.at[k, pl.ds(pl.multiple_of(core * HALF + me // 2 * SLICE, 16), SLICE)]
+            place = wg.at[k, pl.ds(pl.multiple_of(core * HALF + pair * SLICE, 16), SLICE)]
             place[...] = (part * scale).astype(jnp.bfloat16)
-            for t in range(1, group // 2):
-                pltpu.make_async_remote_copy(
-                    src_ref=place, dst_ref=place, send_sem=ag_send.at[k], recv_sem=ag_recv.at[k],
-                    device_id=at(lax.rem(me + 2 * t, group)), device_id_type=pl.DeviceIdType.MESH,
-                ).start()
+            for s in range(8):
+                g = lax.rem(gy + s, 8)
+                for m in range(2):
+                    if s or m:
+                        pltpu.make_async_remote_copy(
+                            src_ref=place, dst_ref=place, send_sem=ag_send.at[k], recv_sem=ag_recv.at[k],
+                            device_id={"gx": z * SUB + lax.rem(y_lo + m, 2) * 2 + core, "gy": g},
+                            device_id_type=pl.DeviceIdType.MESH,
+                        ).start()
 
     def gather_pair(k):
         for here, count in ((me < reducers, SLICES - 1), (me >= reducers, SLICES)):
@@ -387,7 +388,6 @@
     kernel_grad(2, a2, ct)
     two_rows(ft, cb)
     sum_pair(2)
-    send_out(feat, feat_out, 0)
     back2, back1 = backward(ct, h2, u2, r1), backward(u2, h1, u1, r0)
     wait_halo(ct, *PIECES[0], 1)
     conv(ct, cb, ft, 2, centre, False, back2)
@@ -400,6 +400,7 @@
     wait_halo(ct, *PIECES[2], 3)
     conv(ct, cb, ft, 2, sides(64, 32), True, back2)
     sum_pair(0)
+    send_out(feat, feat_out, 0)
     conv(r1, cb, ft, 1, sides(0, 32), True, back1)
     conv(r0, cb, ft, 0, centre, False, backward(u1, h0, None, grad))
     send_out(grad, grad_out, 1)

time: 72.1 us -> 69.7 us (0.967)
  Pallas kernels: 71.4 us -> 69 us
    pallas_call x1, Pallas kernels: 68.7 us -> 66.3 us  [shards(): pl.pallas_call(body, out_shape=(jax.ShapeDtypeStruct(image.shape, bf), ja...]
where the time goes in v3:
time: 69.7 us; the launch traced here: 69.6 us
  Pallas kernels  69 us (99%)
    pallas_call x1, Pallas kernels, shards(): pl.pallas_call(body, out_shape=(jax.ShapeDtypeStruct(image.shape, bf), ja...  66.3 us
    pallas_call x1, Pallas kernels, shards(): pl.pallas_call(finish, out_shape=(jax.ShapeDtypeStruct(image.shape, bf),...  2.64 us

profile of v3, /device:TPU:1, one launch (start us, length us, event | category | flops | bytes accessed | tf_op | source)
XLA Modules:
  0.0 69.6 jit_solution(18049662614361159712)
XLA Ops:
  0.6 66.3 %shard_map.58 = (bf16[32,64,128]{2,1,0:T(8,128)(2,1)}, bf16[32,64,128]{2,1,0:T(8,128)(2,1)}, bf16[3,1152,128]{2,1,0:T(8,128)(2,1)}) custom-call(bf16[32,64,128]{2,1,0:T(8,128)(2,1)} %image.1, bf16[32,64,128]{2,1,0:T(8,128)(2,1)} %cotangent.1, bf16[3,3,3,128,128]{4,3,2,1,0:T(8,128)(2,1)} %weights.1), custom_call_target="tpu_custom_call" | custom-call | tf_op jit(solution)/shard_map/pallas_call | solution.py:484
  67.0 2.6 %shard_map.59 = (bf16[32,64,128]{2,1,0:T(8,128)(2,1)}, bf16[32,64,128]{2,1,0:T(8,128)(2,1)}, f32[3,1152,128]{2,1,0:T(8,128)}) custom-call(bf16[32,64,128]{2,1,0:T(8,128)(2,1)} %get-tuple-element.9.feat_in, bf16[32,64,128]{2,1,0:T(8,128)(2,1)} %get-tuple-element.10.grad_in, bf16[3,1152,128]{2,1,0:T(8,128)(2,1)} %get-tuple-element.11.wg_in), custom_call_target="tpu_custom_call" | custom-call | tf_op jit(solution)/shard_map/pallas_call | solution.py:517
